TPU v7x, 128 devices: a whole 4x4x4 slice. The times are simulated.
128 devices in a mesh: dp: 16 (over x, z), pipe: 4 (over y_lo, core), tensor: 2 (over y_hi).
Axes of the slice: x: 4, y: 4 (y_hi: 2, y_lo: 2; y = y_hi * 2 + y_lo), z: 4, core: 2. Of those that a mesh axis runs over, the one named last changes fastest.
Arguments:
- stream: bfloat16 [4, 4096, 8192], P('pipe', 'dp', 'tensor'), as said below
- backup_stream: bfloat16 [4, 4096, 8192], P('pipe', 'dp', 'tensor'), as said below
- norm_gain: float32 [8192], P('tensor'), may hold values from 0.5 to 2
- w_key: bfloat16 [4, 8192, 1024], P('pipe', None, 'tensor'), may hold values from -0.0625 to 0.0625
- w_value: bfloat16 [4, 8192, 1024], P('pipe', None, 'tensor'), may hold values from -0.0625 to 0.0625
- key_cot: bfloat16 [4, 4096, 1024], P('pipe', 'dp', 'tensor'), as said below
- value_cot: bfloat16 [4, 4096, 1024], P('pipe', 'dp', 'tensor'), as said below
- backup_key_cot: bfloat16 [4, 4096, 1024], P('pipe', 'dp', 'tensor'), as said below
- backup_value_cot: bfloat16 [4, 4096, 1024], P('pipe', 'dp', 'tensor'), as said below
- positions: int32 [4, 4096], P('pipe'), may hold values from 0 to 4095, as said below
- failed: int32 [4], replicated, may hold values from 0 to 15, as said below
- reroute_plan: int32 [4, 32], replicated, may hold values from 0 to 15, as said below
Outputs:
- grad_key: float32 [4, 8192, 1024], P('pipe', 'dp', 'tensor')
- grad_value: float32 [4, 8192, 1024], P('pipe', 'dp', 'tensor')
- stream_grad: bfloat16 [4, 4096, 8192], P('pipe', 'dp', 'tensor')
- spill_grad: bfloat16 [4, 768, 8192], P('pipe', 'dp', 'tensor')
Inputs may be any that keep to these rules, and one draw needn't show every extreme that they name: failed[s] is the replica of section s that has failed; some section has lost replica 0 and some other section replica 16 - 1. reroute_plan[s, b] never equals failed[s]; every other replica takes at least one block of each section, none more than 6, and some replica takes exactly 6. positions count from 0 at each document start; documents of a section's rows start at least every 4096 rows, and in some section exactly every 4096 rows. In stream[j] the rows of replica failed[(j + 1) mod 4] are zero. In backup_stream[s] only the rows of replica (failed[s] + 1) mod 16 are nonzero. In key_cot[s] the rows of replica failed[s] are zero. In value_cot[s] the rows of replica failed[s] are zero. In backup_key_cot[s] only the rows of replica (failed[s] + 1) mod 16 are nonzero. In backup_value_cot[s] only the rows of replica (failed[s] + 1) mod 16 are nonzero.
All inputs are finite; a program needn't handle non-finite values.
Results may differ from a plain program's by a relative error of at most 0.015.
Values may be sent and summed in bfloat16 or wider, within the bound.
No kernel may reach another device: no remote copies, remote signals or barrier semaphores. Data moves between devices by JAX's collectives and lax.ppermute only.
A program may use at most 128 MiB of HBM per device.

v0:
```python
import math
import jax
import jax.numpy as jnp
from jax import lax
from jax.sharding import PartitionSpec as P

D = 8192
HEAD = 128
BLOCK = 8
EPSILON = 1e-05
ROPE_BASE = 500000.0


def passed_along(block, axis, distance):
    devices = range(lax.axis_size(axis))
    route = [((i - distance) % len(devices), i) for i in devices]
    return lax.ppermute(block, axis, route)


def broadcast(shard, axis, root):
    mine = lax.axis_index(axis) == root
    return lax.psum(jnp.where(mine, shard, jnp.zeros_like(shard)), axis)


def frequencies():
    index_half = jnp.arange(HEAD // 2, dtype=jnp.float32)
    return jnp.exp(-(2.0 * index_half / HEAD) * math.log(ROPE_BASE))


def derotate(cotangent, position):
    row_count = cotangent.shape[0]
    pieces = cotangent.astype(jnp.float32).reshape(row_count, -1, 2, HEAD // 2)
    angles = position.astype(jnp.float32)[:, None] * frequencies()[None, :]
    cosine = jnp.cos(angles)[:, None, :]
    sine_values = jnp.sin(angles)[:, None, :]
    lower_half = pieces[:, :, 0, :]
    upper_half = pieces[:, :, 1, :]
    new_lower = lower_half * cosine + upper_half * sine_values
    new_upper = upper_half * cosine - lower_half * sine_values
    return jnp.stack([new_lower, new_upper], axis=2).reshape(row_count, -1).astype(jnp.bfloat16)


def slot_rows(plan_row, owners, capacity_blocks, block_size):
    block_count = plan_row.shape[0]
    block_ids = jnp.arange(block_count, dtype=jnp.int32)
    same_owner = plan_row[:, None] == plan_row[None, :]
    earlier = block_ids[None, :] < block_ids[:, None]
    block_rank = jnp.sum(jnp.where(same_owner & earlier, 1, 0), axis=1).astype(jnp.int32)
    slot_ids = jnp.arange(capacity_blocks, dtype=jnp.int32)
    matches = (plan_row[None, None, :] == owners[:, None, None]) & (
        block_rank[None, None, :] == slot_ids[None, :, None]
    )
    chosen = jnp.sum(jnp.where(matches, block_ids[None, None, :], 0), axis=2)
    filled = jnp.any(matches, axis=2)
    offsets = jnp.arange(block_size, dtype=jnp.int32)
    indices = (chosen[:, :, None] * block_size + offsets[None, None, :]).reshape(
        owners.shape[0], -1
    )
    occupied = jnp.repeat(filled, block_size, axis=1)
    return (indices, occupied)


def on_device(
    stream,
    backup_stream,
    norm_gain,
    w_key,
    w_value,
    key_cot,
    value_cot,
    backup_key_cot,
    backup_value_cot,
    positions,
    failed,
    reroute_plan,
):
    section_idx = lax.axis_index("pipe")
    member = lax.axis_index("dp")
    replicas = lax.axis_size("dp")
    fallen = failed[section_idx]
    keeper = (fallen + 1) % replicas
    plan_row = reroute_plan[section_idx]
    blocks = plan_row.shape[0]
    own_rows = stream.shape[1]
    capacity_blocks = 2 * ((blocks + replicas - 2) // (replicas - 1))
    incoming = passed_along(stream[0], "pipe", 1)
    own_positions = lax.dynamic_slice_in_dim(positions[0], member * own_rows, own_rows, 0)
    dead_positions = lax.dynamic_slice_in_dim(positions[0], fallen * own_rows, own_rows, 0)
    cot_key = derotate(key_cot[0], own_positions)
    cot_both = jnp.concatenate([cot_key, value_cot[0]], axis=1)
    saved_key = derotate(backup_key_cot[0], dead_positions)
    saved_both = jnp.concatenate([saved_key, backup_value_cot[0]], axis=1)
    dead_rows, dead_cots = (
        broadcast(backup_stream[0], "dp", keeper),
        broadcast(saved_both, "dp", keeper),
    )
    indices, occupied = slot_rows(plan_row, jnp.reshape(member, (1,)), capacity_blocks, BLOCK)
    index_list = indices[0]
    keep_slot = occupied[0][:, None]
    survives = member != fallen

    def combine(mine, far_rows):
        picked = jnp.where(
            keep_slot, jnp.take(far_rows, index_list, axis=0), jnp.zeros((), far_rows.dtype)
        )
        kept = jnp.where(survives, mine, jnp.zeros((), mine.dtype))
        return jnp.concatenate([kept, picked], axis=0)

    inputs = combine(incoming, dead_rows)
    cots = combine(cot_both, dead_cots)
    key_width = w_key.shape[2]
    values = inputs.astype(jnp.float32)
    squares = lax.psum(jnp.sum(values * values, axis=1), "tensor")
    scales = lax.rsqrt(squares / D + EPSILON)
    normed = (values * scales[:, None] * norm_gain).astype(jnp.bfloat16)
    partial_sum = lax.dot_general(
        lax.all_gather(normed, "tensor", axis=1, tiled=True),
        cots,
        (((0,), (0,)), ((), ())),
        preferred_element_type=jnp.float32,
    )
    weight_sum = lax.psum_scatter(
        partial_sum.astype(jnp.bfloat16), "dp", scatter_dimension=0, tiled=True
    ).astype(jnp.float32)
    contract = (((1,), (1,)), ((), ()))
    feature = lax.dot_general(
        cots[:, :key_width], w_key[0], contract, preferred_element_type=jnp.float32
    )
    feature = feature + lax.dot_general(
        cots[:, key_width:], w_value[0], contract, preferred_element_type=jnp.float32
    )
    feature_part = lax.psum_scatter(
        feature.astype(jnp.bfloat16), "tensor", scatter_dimension=1, tiled=True
    ).astype(jnp.float32)
    scaled = norm_gain * feature_part
    input_grad = (scales[:, None] * scaled).astype(jnp.bfloat16)
    returned = passed_along(input_grad, "pipe", -1)
    own_count = returned.shape[0] - index_list.shape[0]
    return (
        weight_sum[:, :key_width][None],
        weight_sum[:, key_width:][None],
        returned[:own_count][None],
        returned[own_count:][None],
    )


def solution(mesh):
    return jax.shard_map(
        on_device,
        mesh=mesh,
        in_specs=(
            P("pipe", "dp", "tensor"),
            P("pipe", "dp", "tensor"),
            P("tensor"),
            P("pipe", None, "tensor"),
            P("pipe", None, "tensor"),
            P("pipe", "dp", "tensor"),
            P("pipe", "dp", "tensor"),
            P("pipe", "dp", "tensor"),
            P("pipe", "dp", "tensor"),
            P("pipe", None),
            P(),
            P(),
        ),
        out_specs=(
            P("pipe", "dp", "tensor"),
            P("pipe", "dp", "tensor"),
            P("pipe", "dp", "tensor"),
            P("pipe", "dp", "tensor"),
        ),
        check_vma=False,
    )
```

profile of v0, /device:TPU:1, one launch (start us, length us, event | category | flops | bytes accessed | tf_op | source)
XLA Modules:
  0.0 429.3 jit_solution(5361297684138172872)
XLA Ops:
  7.2 0.0 copy-start.1
  7.2 0.0 all-reduce.3.cloned.1.call-start
  7.2 1.4 dynamic_slice.12
  10.0 1.1 copy.21
  11.1 1.1 copy.23
  12.2 0.7 dynamic-slice_convert_fusion.1
  12.9 0.5 multiply_cosine_fusion.1
  13.5 0.1 add_convert_fusion
  13.6 0.0 copy-start.2
  13.7 0.1 copy.24
  13.8 0.0 copy-done.1
  13.8 1.5 select_bitcast_fusion
  15.3 1.9 maximum_select_fusion.1
  17.1 0.0 all-reduce.3.cloned.1.call-update
  17.2 0.0 reduce-scatter.5.cloned.1.call-start
  17.9 0.7 broadcast_compare_fusion
  18.6 0.2 select_reduce_fusion
  18.7 0.2 select_reduce_fusion.1
  19.0 0.1 add.107
  19.0 0.1 add.116
  19.1 0.1 add.108
  19.2 0.2 fusion.13
  19.4 0.1 broadcast_in_dim.115
  19.5 0.1 broadcast_in_dim.116
  19.6 0.1 add.118
  19.7 0.1 add.110
  19.8 0.1 copy.22
  20.0 0.0 copy-done.2
  20.0 0.1 maximum_select_fusion
  20.1 93.1 %all-reduce.3.cloned.1.call-done = (bf16[256,4096]{1,0:T(8,128)(2,1)}, bf16[256,1024]{1,0:T(8,128)(2,1)}) async-done(((bf16[256,4096]{1,0:T(8,128)(2,1)}, bf16[256,1024]{1,0:T(8,128)(2,1)}), (bf16[256,4096]{1,0:T(8,128)(2,1)}, bf16[256,1024]{1,0:T(8,128)(2,1)})) %all-reduce.3.cloned.1.call-update) | async-done | bytes 2621456 | tf_op jit(solution)/shard_map/psum | solution.py:22
  113.2 1.8 gather_fusion.1
  115.0 0.1 select_select_fusion.1
  115.1 11.4 %fusion.2 = f32[304,8192]{1,0:T(8,128)} fusion(bf16[1,8192,512]{2,1,0:T(8,128)(2,1)} %param.15, bf16[256,1024]{1,0:T(8,128)(2,1)S(1)} %maximum_select_fusion, bf16[48,1024]{1,0:T(8,128)(2,1)S(1)} %select_select_fusion.1), kind=kOutput, calls=%fused_computation.6 | convolution fusion | flops 2550759424 | bytes 18972672 | tf_op jit(solution)/shard_map/dot_general | solution.py:126
  126.5 12.1 %fusion = bf16[304,8192]{1,0:T(8,128)(2,1)} fusion(f32[304,8192]{1,0:T(8,128)} %fusion.2, bf16[1,8192,512]{2,1,0:T(8,128)(2,1)} %param.16, bf16[256,1024]{1,0:T(8,128)(2,1)S(1)} %maximum_select_fusion, bf16[48,1024]{1,0:T(8,128)(2,1)S(1)} %select_select_fusion.1), kind=kOutput, calls=%fused_computation.4 | convolution fusion | flops 2555740160 | bytes 23953408 | tf_op jit(solution)/shard_map/dot_general | solution.py:129
  138.6 0.0 copy-start.4
  138.6 0.0 reduce-scatter.5.cloned.1.call-update
  138.6 0.0 all-gather.2.cloned.1.call-start
  138.7 1.5 copy-done.4
  140.2 0.0 copy-start.3
  140.2 2.1 collective-permute-start
  142.4 59.5 %collective-permute-done = bf16[256,4096]{1,0:T(8,128)(2,1)S(1)} collective-permute-done((bf16[256,4096]{1,0:T(8,128)(2,1)S(1)}, bf16[256,4096]{1,0:T(8,128)(2,1)S(1)}, u32[]{:S(2)}, u32[]{:S(2)}) %collective-permute-start) | collective-permute-done | bytes 2097184 | tf_op jit(solution)/shard_map/ppermute | solution.py:17
  201.8 0.1 broadcast_select_fusion
  201.9 3.0 gather_fusion
  205.0 0.1 select_select_fusion
  205.1 0.6 fusion.4
  205.7 5.7 %psum.22 = f32[304]{0:T(512)S(1)} all-reduce(f32[304]{0:T(512)S(1)} %fusion.4), channel_id=1, replica_groups=mesh['dp'=16,'pipe'=4,'tensor'=2] {'tensor'}, use_global_device_ids=true, to_apply=%region_5.6 | all-reduce | flops 304 | bytes 2432 | tf_op jit(solution)/shard_map/psum | solution.py:113
  211.5 12.0 %reduce-scatter.5.cloned.1.call-done = bf16[304,4096]{1,0:T(8,128)(2,1)} async-done(((bf16[304,8192]{1,0:T(8,128)(2,1)}), bf16[304,4096]{1,0:T(8,128)(2,1)}) %reduce-scatter.5.cloned.1.call-update) | async-done | bytes 2490384 | tf_op jit(solution)/shard_map/reduce_scatter | solution.py:132
  223.4 0.0 copy-done.3
  223.4 4.9 %multiply_convert_fusion = (bf16[304,4096]{1,0:T(8,128)(2,1)}, bf16[304,4096]{1,0:T(8,128)(2,1)}) fusion(bf16[304,4096]{1,0:T(8,128)(2,1)} %reduce-scatter.5.cloned.1.call-done, f32[4096]{0:T(1024)S(1)} %copy-done.3, f32[304]{0:T(512)S(1)} %add_rsqrt_fusion, bf16[48,4096]{1,0:T(8,128)(2,1)S(1)} %select_select_fusion, ...), kind=kLoop, calls=%fused_computation.13 | loop fusion | flops 13697024 | bytes 9979072 | tf_op jit(solution)/shard_map/convert_element_type | solution.py:136
  228.3 0.0 all-gather.2.cloned.1.call-update
  228.3 0.2 reduce-scatter.3.cloned.1.call-start
  228.5 66.4 %all-gather.2.cloned.1.call-done = bf16[304,8192]{1,0:T(8,128)(2,1)} async-done(((bf16[304,4096]{1,0:T(8,128)(2,1)}), bf16[304,8192]{1,0:T(8,128)(2,1)}) %all-gather.2.cloned.1.call-update) | async-done | bytes 4980752 | tf_op jit(solution)/shard_map/all_gather | solution.py:117
  294.9 14.9 %convolution_convert_fusion = bf16[8192,1024]{1,0:T(8,128)(2,1)} fusion(bf16[304,8192]{1,0:T(8,128)(2,1)} %all-gather.2.cloned.1.call-done, bf16[48,1024]{1,0:T(8,128)(2,1)S(1)} %select_select_fusion.1, bf16[256,1024]{1,0:T(8,128)(2,1)S(1)} %maximum_select_fusion), kind=kOutput, calls=%fused_computation.2 | convolution fusion | flops 5109907456 | bytes 22380544 | tf_op jit(solution)/shard_map/dot_general | solution.py:116
  309.8 0.0 copy-start
  309.8 0.0 reduce-scatter.3.cloned.1.call-update
  309.9 1.7 copy-done
  311.6 0.7 collective-permute-start.1
  312.2 29.4 %collective-permute-done.1 = bf16[304,4096]{1,0:T(8,128)(2,1)S(1)} collective-permute-done((bf16[304,4096]{1,0:T(8,128)(2,1)S(1)}, bf16[304,4096]{1,0:T(8,128)(2,1)S(1)}, u32[]{:S(2)}, u32[]{:S(2)}) %collective-permute-start.1) | collective-permute-done | bytes 2490400 | tf_op jit(solution)/shard_map/ppermute | solution.py:17
  341.6 0.8 slice_bitcast_fusion.3
  342.4 1.5 slice_bitcast_fusion
  343.8 76.0 %reduce-scatter.3.cloned.1.call-done = bf16[512,1024]{1,0:T(8,128)(2,1)} async-done(((bf16[8192,1024]{1,0:T(8,128)(2,1)}), bf16[512,1024]{1,0:T(8,128)(2,1)}) %reduce-scatter.3.cloned.1.call-update) | async-done | bytes 1048592 | tf_op jit(solution)/shard_map/reduce_scatter | solution.py:122
  419.8 1.5 convert_element_type.76
  421.3 1.5 slice_bitcast_fusion.1
  (12 shorter events, 0.2 us)
Async XLA Ops:
  7.2 6.7 %copy-start.1 = (bf16[1,256,4096]{2,1,0:T(8,128)(2,1)S(1)}, bf16[1,256,4096]{2,1,0:T(8,128)(2,1)}, u32[]{:S(2)}) copy-start(bf16[1,256,4096]{2,1,0:T(8,128)(2,1)} %param.13) | copy-start | bytes 6291460
  7.2 106.0 %all-reduce.3.cloned.1.call-start = ((), (), s32[]{:S(2)}) async-start(), calls=%async_computation.5 | async-start | bytes 5242880 | tf_op jit(solution)/shard_map/psum | solution.py:22
  13.6 6.3 %copy-start.2 = (bf16[1,256,512]{2,1,0:T(8,128)(2,1)S(1)}, bf16[1,256,512]{2,1,0:T(8,128)(2,1)}, u32[]{:S(2)}) copy-start(bf16[1,256,512]{2,1,0:T(8,128)(2,1)} %param.18) | copy-start | bytes 786436
  17.2 206.2 %reduce-scatter.5.cloned.1.call-start = ((), (), s32[]{:S(2)}) async-start(), calls=%async_computation.4 | async-start | bytes 7471104 | tf_op jit(solution)/shard_map/reduce_scatter | solution.py:132
  138.6 1.6 copy-start.4
  138.6 156.3 %all-gather.2.cloned.1.call-start = ((), (), s32[]{:S(2)}) async-start(), calls=%async_computation.2 | async-start | bytes 7471104 | tf_op jit(solution)/shard_map/all_gather | solution.py:117
  140.2 83.2 %copy-start.3 = (f32[4096]{0:T(1024)S(1)}, f32[4096]{0:T(1024)}, u32[]{:S(2)}) copy-start(f32[4096]{0:T(1024)} %param.14) | copy-start | bytes 49156
  140.2 61.6 %collective-permute-start = (bf16[256,4096]{1,0:T(8,128)(2,1)S(1)}, bf16[256,4096]{1,0:T(8,128)(2,1)S(1)}, u32[]{:S(2)}, u32[]{:S(2)}) collective-permute-start(bf16[256,4096]{1,0:T(8,128)(2,1)S(1)} %bitcast.46), channel_id=1, source_target_pairs={{6,0},{0,2},{2,4},{4,6},{7,1},{1,3},{3,5},{5,7},{14,8},{8,10},{10,... | collective-permute-start | bytes 6291464 | tf_op jit(solution)/shard_map/ppermute | solution.py:17
  228.3 191.5 %reduce-scatter.3.cloned.1.call-start = ((), (), s32[]{:S(2)}) async-start(), calls=%async_computation.3 | async-start | bytes 17825792 | tf_op jit(solution)/shard_map/reduce_scatter | solution.py:122
  309.8 1.7 copy-start
  311.6 30.1 %collective-permute-start.1 = (bf16[304,4096]{1,0:T(8,128)(2,1)S(1)}, bf16[304,4096]{1,0:T(8,128)(2,1)S(1)}, u32[]{:S(2)}, u32[]{:S(2)}) collective-permute-start(bf16[304,4096]{1,0:T(8,128)(2,1)S(1)} %copy-done), channel_id=1, source_target_pairs={{2,0},{4,2},{6,4},{0,6},{3,1},{5,3},{7,5},{1,7},{10,8},{12,10},{14... | collective-permute-start | bytes 7471112 | tf_op jit(solution)/shard_map/ppermute | solution.py:17
Sparse Core Ops, SparseCore 0:
  17.3 95.8 all-reduce.2
  138.8 84.5 reduce-scatter.4
  228.4 66.4 all-gather.1
  310.0 109.7 reduce-scatter.2
where the time goes:
time: 430 us; the launch traced here: 429 us
  waiting for transfers between devices  336 us (78%)
  matrix products  38.4 us (9%)
  local copies, waits for them, and re-layouts  16.2 us (4%)
  between operations  16 us (4%)
  other arithmetic  13.5 us (3%)
  blocking collectives  5.75 us (1%)
    psum x1, waiting for transfers between devices, broadcast(): return lax.psum(jnp.where(mine, shard, jnp.zeros_like(shard)), axis)  93.1 us
    ppermute x2, waiting for transfers between devices, passed_along(): return lax.ppermute(block, axis, route)  88.9 us
    reduce_scatter x1, waiting for transfers between devices, on_device(): lax.psum_scatter(partial_sum.astype(jnp.bfloat16), 'dp', scatter_dimensio...  76 us
    all_gather x1, waiting for transfers between devices, on_device(): lax.all_gather(normed, 'tensor', axis=1, tiled=True)  66.4 us
    dot_general x1, matrix products, on_device(): lax.dot_general(lax.all_gather(normed, 'tensor', axis=1, tiled=True), cot...  14.9 us
    dot_general x1, matrix products, on_device(): lax.dot_general(cots[:, key_width:], w_value[0], contract, preferred_elem...  12.1 us
    reduce_scatter x1, waiting for transfers between devices, on_device(): lax.psum_scatter(feature.astype(jnp.bfloat16), 'tensor', scatter_dimensio...  12 us
    dot_general x1, matrix products, on_device(): lax.dot_general(cots[:, :key_width], w_key[0], contract, preferred_elemen...  11.4 us
  transfers between devices with their start and end apart: 6, of which 6 were waited for; matrix products, arithmetic and copies ran while one was open for 2% of the time, Pallas kernels for 0%

commit v1 on v0

--- a/solution.py
+++ b/solution.py
@@ -11,6 +11,12 @@
 ROPE_BASE = 500000.0
 
 
+def gather_and_add(x, axis):
+    terms = lax.all_gather(x, axis, axis=0, tiled=False)
+    total = terms.sum(axis=0)
+    return total
+
+
 def passed_along(block, axis, distance):
     devices = range(lax.axis_size(axis))
     route = [((i - distance) % len(devices), i) for i in devices]
@@ -19,7 +25,7 @@
 
 def broadcast(shard, axis, root):
     mine = lax.axis_index(axis) == root
-    return lax.psum(jnp.where(mine, shard, jnp.zeros_like(shard)), axis)
+    return gather_and_add(jnp.where(mine, shard, jnp.zeros_like(shard)), axis)
 
 
 def frequencies():

time: 430 us -> 569 us (1.32)
  waiting for transfers between devices: 336 us -> 454 us
  other arithmetic: 13.5 us -> 31.9 us
    all_gather x0 -> x2, waiting for transfers between devices: none -> 212 us  [gather_and_add(): terms = lax.all_gather(x, axis, axis=0, tiled=False)]
    psum x1 -> x0, waiting for transfers between devices: 93.1 us -> none  [broadcast(): return lax.psum(jnp.where(mine, shard, jnp.zeros_like(shard)), axis)]
    ppermute x2, waiting for transfers between devices: 88.9 us -> 52.4 us  [passed_along(): return lax.ppermute(block, axis, route)]
    reduce_scatter x1, waiting for transfers between devices: 12 us -> 44.8 us  [on_device(): lax.psum_scatter(feature.astype(jnp.bfloat16), 'tensor', scatter_dimensio...]
    reduce_sum x0 -> x2, other arithmetic: none -> 18.4 us  [gather_and_add(): total = terms.sum(axis=0)]
  transfers between devices with their start and end apart: 6 -> 7, of which waited for: 6 -> 7; matrix products, arithmetic and copies ran while one was open for 2% -> 10% of each run, Pallas kernels for 0% -> 0%
where the time goes in v1:
time: 569 us; the launch traced here: 568 us
  waiting for transfers between devices  454 us (80%)
  matrix products  38.8 us (7%)
  other arithmetic  31.9 us (6%)
  local copies, waits for them, and re-layouts  18.9 us (3%)
  between operations  16 us (3%)
  blocking collectives  5.75 us (1%)
    all_gather x2, waiting for transfers between devices, gather_and_add(): terms = lax.all_gather(x, axis, axis=0, tiled=False)  212 us
    reduce_scatter x1, waiting for transfers between devices, on_device(): lax.psum_scatter(partial_sum.astype(jnp.bfloat16), 'dp', scatter_dimensio...  75.9 us
    all_gather x1, waiting for transfers between devices, on_device(): lax.all_gather(normed, 'tensor', axis=1, tiled=True)  69.2 us
    ppermute x2, waiting for transfers between devices, passed_along(): return lax.ppermute(block, axis, route)  52.4 us
    reduce_scatter x1, waiting for transfers between devices, on_device(): lax.psum_scatter(feature.astype(jnp.bfloat16), 'tensor', scatter_dimensio...  44.8 us
    reduce_sum x2, other arithmetic, gather_and_add(): total = terms.sum(axis=0)  18.4 us
    dot_general x1, matrix products, on_device(): lax.dot_general(lax.all_gather(normed, 'tensor', axis=1, tiled=True), cot...  15 us
    dot_general x1, matrix products, on_device(): lax.dot_general(cots[:, key_width:], w_value[0], contract, preferred_elem...  12.4 us
  transfers between devices with their start and end apart: 7, of which 7 were waited for; matrix products, arithmetic and copies ran while one was open for 10% of the time, Pallas kernels for 0%

profile of v1, /device:TPU:1, one launch (start us, length us, event | category | flops | bytes accessed | tf_op | source)
XLA Modules:
  0.0 567.9 jit_solution(16384293832523765125)
XLA Ops:
  7.2 0.0 copy-start.1
  7.2 0.0 all-gather.8.cloned.1.call-start
  7.2 1.4 dynamic_slice.12
  10.0 1.1 copy.30
  11.1 1.1 copy.32
  12.2 1.1 copy.33
  13.3 0.7 dynamic-slice_convert_fusion.1
  14.0 0.5 multiply_cosine_fusion.1
  14.6 0.8 add_convert_fusion
  15.4 0.1 maximum_select_fusion.1
  15.5 1.0 copy.34
  16.5 0.0 all-gather.8.cloned.1.call-update
  16.5 0.0 all-gather.4.cloned.1.call-start
  16.6 0.0 copy-done.1
  16.6 1.5 broadcast_select_fusion
  18.1 0.0 all-gather.4.cloned.1.call-update
  18.1 0.0 reduce-scatter.5.cloned.1.call-start
  18.8 0.7 broadcast_compare_fusion
  19.5 0.2 select_reduce_fusion
  19.6 0.2 select_reduce_fusion.1
  19.9 0.1 add.103
  19.9 0.1 add.112
  20.0 0.1 add.104
  20.1 0.2 fusion.12
  20.3 0.1 broadcast_in_dim.117
  20.4 0.1 broadcast_in_dim.118
  20.5 0.1 add.114
  20.6 0.1 add.106
  20.6 1.1 copy.31
  21.8 0.1 maximum_select_fusion
  21.9 68.8 %all-gather.8.cloned.1.call-done = bf16[16,256,1024]{2,1,0:T(8,128)(2,1)} async-done(((bf16[1,256,1024]{2,1,0:T(8,128)(2,1)}), bf16[16,256,1024]{2,1,0:T(8,128)(2,1)}) %all-gather.8.cloned.1.call-update) | async-done | bytes 8388624 | tf_op jit(solution)/shard_map/all_gather | solution.py:15
  90.8 5.4 reduce_sum.55
  96.2 0.7 gather_fusion.1
  96.9 0.1 select_select_fusion.1
  97.0 0.2 copy.37
  97.1 11.4 %fusion.2 = f32[304,8192]{1,0:T(8,128)} fusion(bf16[1,8192,512]{2,1,0:T(8,128)(2,1)} %param.15, bf16[256,1024]{0,1:T(8,128)(2,1)S(1)} %maximum_select_fusion, bf16[48,1024]{0,1:T(8,128)(2,1)S(1)} %copy.37), kind=kOutput, calls=%fused_computation.6 | convolution fusion | flops 2550759424 | bytes 18972672 | tf_op jit(solution)/shard_map/dot_general | solution.py:132
  108.6 12.4 %fusion = bf16[304,8192]{1,0:T(8,128)(2,1)} fusion(f32[304,8192]{1,0:T(8,128)} %fusion.2, bf16[1,8192,512]{2,1,0:T(8,128)(2,1)} %param.16, bf16[256,1024]{0,1:T(8,128)(2,1)S(1)} %maximum_select_fusion, bf16[48,1024]{0,1:T(8,128)(2,1)S(1)} %copy.37), kind=kOutput, calls=%fused_computation.4 | convolution fusion | flops 2555740160 | bytes 23953408 | tf_op jit(solution)/shard_map/dot_general | solution.py:135
  121.0 0.0 reduce-scatter.5.cloned.1.call-update
  121.0 0.0 all-gather.6.cloned.1.call-start
  121.0 1.6 copy-done.4
  122.6 1.7 collective-permute-start
  124.3 23.0 %collective-permute-done = bf16[256,4096]{1,0:T(8,128)(2,1)S(1)} collective-permute-done((bf16[256,4096]{1,0:T(8,128)(2,1)S(1)}, bf16[256,4096]{1,0:T(8,128)(2,1)S(1)}, u32[]{:S(2)}, u32[]{:S(2)}) %collective-permute-start) | collective-permute-done | bytes 2097184 | tf_op jit(solution)/shard_map/ppermute | solution.py:23
  147.3 0.1 broadcast_select_fusion.1
  147.5 142.8 %all-gather.4.cloned.1.call-done = bf16[16,256,4096]{2,1,0:T(8,128)(2,1)} async-done(((bf16[1,256,4096]{2,1,0:T(8,128)(2,1)}), bf16[16,256,4096]{2,1,0:T(8,128)(2,1)}) %all-gather.4.cloned.1.call-update) | async-done | bytes 33554448 | tf_op jit(solution)/shard_map/all_gather | solution.py:15
  290.3 13.0 %reduce_sum.53 = bf16[256,4096]{1,0:T(8,128)(2,1)} reduce(bf16[16,256,4096]{2,1,0:T(8,128)(2,1)} %all-gather.4.cloned.1.call-done, bf16[]{:T(256)} %constant.70.clone.1), dimensions={0}, to_apply=%region_3.4 | reduce | flops 15728640 | bytes 35651584 | tf_op jit(solution)/shard_map/reduce_sum | solution.py:16
  303.3 3.8 gather_fusion
  307.0 1.1 select_select_fusion
  308.2 0.6 fusion.4
  308.7 5.7 %psum.7 = f32[304]{0:T(512)S(1)} all-reduce(f32[304]{0:T(512)S(1)} %fusion.4), channel_id=1, replica_groups=mesh['dp'=16,'pipe'=4,'tensor'=2] {'tensor'}, use_global_device_ids=true, to_apply=%region_5.6 | all-reduce | flops 304 | bytes 2432 | tf_op jit(solution)/shard_map/psum | solution.py:119
  314.5 44.8 %reduce-scatter.5.cloned.1.call-done = bf16[304,4096]{1,0:T(8,128)(2,1)} async-done(((bf16[304,8192]{1,0:T(8,128)(2,1)}), bf16[304,4096]{1,0:T(8,128)(2,1)}) %reduce-scatter.5.cloned.1.call-update) | async-done | bytes 2490384 | tf_op jit(solution)/shard_map/reduce_scatter | solution.py:138
  359.3 4.9 multiply_convert_fusion
  364.2 0.0 all-gather.6.cloned.1.call-update
  364.3 0.0 reduce-scatter.3.cloned.1.call-start
  364.3 69.2 %all-gather.6.cloned.1.call-done = bf16[304,8192]{1,0:T(8,128)(2,1)} async-done(((bf16[304,4096]{1,0:T(8,128)(2,1)}), bf16[304,8192]{1,0:T(8,128)(2,1)}) %all-gather.6.cloned.1.call-update) | async-done | bytes 4980752 | tf_op jit(solution)/shard_map/all_gather | solution.py:123
  433.5 15.0 %convolution_convert_fusion = bf16[8192,1024]{1,0:T(8,128)(2,1)} fusion(bf16[304,8192]{1,0:T(8,128)(2,1)} %all-gather.6.cloned.1.call-done, bf16[48,1024]{0,1:T(8,128)(2,1)S(1)} %copy.37, bf16[256,1024]{0,1:T(8,128)(2,1)S(1)} %maximum_select_fusion), kind=kOutput, calls=%fused_computation.2 | convolution fusion | flops 5109907456 | bytes 22380544 | tf_op jit(solution)/shard_map/dot_general | solution.py:122
  448.5 0.0 reduce-scatter.3.cloned.1.call-update
  448.5 1.7 copy-done
  450.2 0.7 collective-permute-start.1
  450.8 29.4 %collective-permute-done.1 = bf16[304,4096]{1,0:T(8,128)(2,1)S(1)} collective-permute-done((bf16[304,4096]{1,0:T(8,128)(2,1)S(1)}, bf16[304,4096]{1,0:T(8,128)(2,1)S(1)}, u32[]{:S(2)}, u32[]{:S(2)}) %collective-permute-start.1) | collective-permute-done | bytes 2490400 | tf_op jit(solution)/shard_map/ppermute | solution.py:23
  480.2 0.8 slice_bitcast_fusion.3
  481.0 1.5 slice_bitcast_fusion
  482.5 75.9 %reduce-scatter.3.cloned.1.call-done = bf16[512,1024]{1,0:T(8,128)(2,1)} async-done(((bf16[8192,1024]{1,0:T(8,128)(2,1)}), bf16[512,1024]{1,0:T(8,128)(2,1)}) %reduce-scatter.3.cloned.1.call-update) | async-done | bytes 1048592 | tf_op jit(solution)/shard_map/reduce_scatter | solution.py:128
  558.4 1.5 convert_element_type.83
  559.8 1.5 slice_bitcast_fusion.1
  (18 shorter events, 0.2 us)
Async XLA Ops:
  7.2 9.4 %copy-start.1 = (bf16[1,256,4096]{2,1,0:T(8,128)(2,1)S(1)}, bf16[1,256,4096]{2,1,0:T(8,128)(2,1)}, u32[]{:S(2)}) copy-start(bf16[1,256,4096]{2,1,0:T(8,128)(2,1)} %param.13) | copy-start | bytes 6291460
  7.2 83.6 %all-gather.8.cloned.1.call-start = ((), (), s32[]{:S(2)}) async-start(), calls=%async_computation.4 | async-start | bytes 8912896 | tf_op jit(solution)/shard_map/all_gather | solution.py:15
  15.4 6.4 %copy-start.2 = (bf16[256,4,1,64]{0,3,2,1:T(8,128)(2,1)S(1)}, bf16[256,4,1,64]{0,3,2,1:T(8,128)(2,1)}, u32[]{:S(2)}) copy-start(bf16[256,4,1,64]{0,3,2,1:T(8,128)(2,1)} %get-tuple-element.23) | copy-start | bytes 393220
  16.5 273.8 %all-gather.4.cloned.1.call-start = ((), (), s32[]{:S(2)}) async-start(), calls=%async_computation.2 | async-start | bytes 35651584 | tf_op jit(solution)/shard_map/all_gather | solution.py:15
  18.1 341.2 %reduce-scatter.5.cloned.1.call-start = ((), (), s32[]{:S(2)}) async-start(), calls=%async_computation.6 | async-start | bytes 7471104 | tf_op jit(solution)/shard_map/reduce_scatter | solution.py:138
  121.0 1.7 copy-start.4
  121.0 312.5 %all-gather.6.cloned.1.call-start = ((), (), s32[]{:S(2)}) async-start(), calls=%async_computation.3 | async-start | bytes 7471104 | tf_op jit(solution)/shard_map/all_gather | solution.py:123
  122.6 24.7 %collective-permute-start = (bf16[256,4096]{1,0:T(8,128)(2,1)S(1)}, bf16[256,4096]{1,0:T(8,128)(2,1)S(1)}, u32[]{:S(2)}, u32[]{:S(2)}) collective-permute-start(bf16[256,4096]{1,0:T(8,128)(2,1)S(1)} %bitcast.42), channel_id=1, source_target_pairs={{6,0},{0,2},{2,4},{4,6},{7,1},{1,3},{3,5},{5,7},{14,8},{8,10},{10,... | collective-permute-start | bytes 6291464 | tf_op jit(solution)/shard_map/ppermute | solution.py:23
  303.3 56.1 %copy-start.3 = (f32[4096]{0:T(1024)S(1)}, f32[4096]{0:T(1024)}, u32[]{:S(2)}) copy-start(f32[4096]{0:T(1024)} %param.14) | copy-start | bytes 49156
  364.3 194.1 %reduce-scatter.3.cloned.1.call-start = ((), (), s32[]{:S(2)}) async-start(), calls=%async_computation.5 | async-start | bytes 17825792 | tf_op jit(solution)/shard_map/reduce_scatter | solution.py:128
  448.5 1.7 copy-start
  450.2 30.1 %collective-permute-start.1 = (bf16[304,4096]{1,0:T(8,128)(2,1)S(1)}, bf16[304,4096]{1,0:T(8,128)(2,1)S(1)}, u32[]{:S(2)}, u32[]{:S(2)}) collective-permute-start(bf16[304,4096]{1,0:T(8,128)(2,1)S(1)} %copy-done), channel_id=1, source_target_pairs={{2,0},{4,2},{6,4},{0,6},{3,1},{5,3},{7,5},{1,7},{10,8},{12,10},{14... | collective-permute-start | bytes 7471112 | tf_op jit(solution)/shard_map/ppermute | solution.py:23
Sparse Core Ops, SparseCore 0:
  16.7 74.0 all-gather.7
  93.5 196.7 all-gather.3
  292.7 66.5 reduce-scatter.4
  364.4 69.0 all-gather.5
  448.6 109.7 reduce-scatter.2
